TPU v7x, 512 devices: a whole 4x8x8 slice. The times are simulated.
512 devices in a mesh: rep: 16 (over z, core), fsdp: 32 (over y, x).
Axes of the slice: x: 4, y: 8, z: 8, core: 2. Of those that a mesh axis runs over, the one named last changes fastest.
Arguments:
- activations: bfloat16 [131072, 6144], P(('rep', 'fsdp')), may hold values from -6 to 6
- unit_grads: bfloat16 [131072, 128], P(('rep', 'fsdp')), may hold values from -0.0625 to 0.0625
- momentum: float32 [16, 6144, 128], P('rep', 'fsdp'), may hold values from -6 to 6
- weights: float32 [6144, 128], P('fsdp'), may hold values from -0.75 to 0.75
- block_ids: int32 [16, 192, 6], P('rep', 'fsdp'), may hold values from 0 to 31, as said below
- block_counts: int32 [16, 192], P('rep', 'fsdp'), may hold values from 1 to 6, as said below
Outputs:
- new_weights: float32 [6144, 128], P('fsdp')
- new_momentum: float32 [16, 6144, 128], P('rep', 'fsdp')
Inputs may be any that keep to these rules, and one draw needn't show every extreme that they name: `block_counts`: every replica has a tile with 6 live slots. `block_ids`: the live slots of a tile name different blocks; slots at or past the count hold 0.
All inputs are finite; a program needn't handle non-finite values.
Results may differ from a plain program's by a relative error of at most 0.0055.
Values may be sent and summed in bfloat16 or wider, within the bound.
A program may use at most 64 MiB of HBM per device.

v0:
```python
import jax
import jax.numpy as jnp
from jax import lax
from jax.sharding import PartitionSpec as P

EDGE = 64
NBLK = 32
SLOTS = 6


def cosine_table(edge):
    freq = jnp.arange(edge, dtype=jnp.float32)[:, None]
    place = jnp.arange(edge, dtype=jnp.float32)[None, :]
    factor = jnp.where(freq == 0, jnp.sqrt(1.0 / edge), jnp.sqrt(2.0 / edge))
    return factor * jnp.cos(jnp.pi * (2.0 * place + 1.0) * freq / (2.0 * edge))


def forward_tiles(moment4, table):
    partial_rows = jnp.einsum("ui,aibj->aubj", table, moment4, precision=lax.Precision.HIGHEST)
    return jnp.einsum("aubj,vj->abuv", partial_rows, table, precision=lax.Precision.HIGHEST)


def inverse_tiles(coeffs4, table):
    partial_rows = jnp.einsum("ui,abuv->aibv", table, coeffs4, precision=lax.Precision.HIGHEST)
    return jnp.einsum("aibv,vj->aibj", partial_rows, table, precision=lax.Precision.HIGHEST)


def on_device(activations, unit_grads, momentum, weights, block_ids, block_counts):
    rows_dev = weights.shape[0]
    width = weights.shape[1]
    rows_a = rows_dev // EDGE
    cols_b = width // EDGE
    tiles_dev = rows_a * cols_b
    table = cosine_table(EDGE)
    gradient = lax.psum_scatter(
        lax.dot_general(
            activations, unit_grads, (((0,), (0,)), ((), ())), preferred_element_type=jnp.float32
        ),
        "fsdp",
        scatter_dimension=0,
        tiled=True,
    )
    moment = 0.9 * momentum[0] + gradient
    coeffs = forward_tiles(moment.reshape(rows_a, EDGE, cols_b, EDGE), table).reshape(
        tiles_dev, NBLK, 128
    )
    blocks = jnp.arange(NBLK, dtype=jnp.int32)
    active = (jnp.arange(SLOTS, dtype=jnp.int32)[None, :] < block_counts[0][:, None]).astype(
        jnp.float32
    )
    onehot = (block_ids[0][:, :, None] == blocks[None, None, :]).astype(jnp.float32) * active[
        :, :, None
    ]
    picked = jnp.einsum("tkn,tnc->tkc", onehot, coeffs, precision=lax.Precision.HIGHEST).astype(
        jnp.bfloat16
    )
    removed = jnp.einsum(
        "tkn,tkc->tnc", onehot, picked.astype(jnp.float32), precision=lax.Precision.HIGHEST
    )
    taken = inverse_tiles(removed.reshape(rows_a, cols_b, EDGE, EDGE), table).reshape(
        rows_dev, width
    )
    new_momentum = moment - taken
    picked_all, chosen_all = (
        lax.all_gather(picked[None], "rep", axis=0, tiled=True),
        lax.all_gather(block_ids, "rep", axis=0, tiled=True),
    )
    onehot_all = (chosen_all[:, :, :, None] == blocks[None, None, None, :]).astype(jnp.float32)
    summed = jnp.einsum(
        "rtkn,rtkc->tnc",
        onehot_all,
        picked_all.astype(jnp.float32),
        precision=lax.Precision.HIGHEST,
    )
    update = inverse_tiles(summed.reshape(rows_a, cols_b, EDGE, EDGE), table)
    spread = jnp.sqrt(jnp.mean(update * update, axis=(1, 3), keepdims=True) + 1e-06)
    new_weights = weights - 0.25 * jnp.tanh(update / spread).reshape(rows_dev, width)
    return (new_weights, new_momentum[None])


def solution(mesh):
    placed = (
        P(("rep", "fsdp"), None),
        P(("rep", "fsdp"), None),
        P("rep", "fsdp", None),
        P("fsdp", None),
        P("rep", "fsdp", None),
        P("rep", "fsdp"),
    )
    return jax.shard_map(
        on_device,
        mesh=mesh,
        in_specs=placed,
        out_specs=(P("fsdp", None), P("rep", "fsdp", None)),
        check_vma=False,
    )
```

profile of v0, /device:TPU:1, one launch (start us, length us, event | category | flops | bytes accessed | tf_op | source)
XLA Modules:
  0.0 282.9 jit_solution(7343349654300801875)
XLA Ops:
  7.2 0.0 reduce-scatter.2.cloned.1.call-start
  7.2 1.8 copy-done
  9.1 3.5 %fusion.48 = f32[6144,128]{1,0:T(8,128)} fusion(bf16[256,6144]{1,0:T(8,128)(2,1)S(1)} %copy-done, bf16[256,128]{1,0:T(8,128)(2,1)} %param.7), kind=kOutput, calls=%fused_computation.66 | convolution fusion | flops 402653184 | bytes 6356992 | tf_op jit(solution)/shard_map/dot_general | solution.py:36
  12.6 0.0 reduce-scatter.2.cloned.1.call-update
  12.6 0.7 copy-done.2
  13.3 24.6 %all_gather.6 = s32[16,6,6]{2,1,0:T(8,128)S(1)} all-gather(s32[1,6,6]{2,1,0:T(8,128)S(1)} %copy.56), channel_id=1, replica_groups=mesh['rep'=16,'fsdp'=32] {'rep'}, dimensions={0}, use_global_device_ids=true | all-gather | bytes 2448 | tf_op jit(solution)/shard_map/all_gather | solution.py:66
  37.9 0.7 copy.28
  38.6 0.1 fusion.38
  38.7 199.1 %reduce-scatter.2.cloned.1.call-done = f32[192,128]{1,0:T(8,128)} async-done(((f32[6144,128]{1,0:T(8,128)}), f32[192,128]{1,0:T(8,128)}) %reduce-scatter.2.cloned.1.call-update) | async-done | bytes 98320 | tf_op jit(solution)/shard_map/reduce_scatter | solution.py:35
  237.9 0.9 bitcast_add_fusion
  238.8 0.2 reshape.75
  238.9 0.5 convolution_bitcast_fusion.3
  239.5 0.4 convolution_bitcast_fusion.2
  239.9 0.8 copy.31
  240.7 1.0 reshape.76
  241.7 0.3 convolution_convert_fusion
  242.0 24.1 %all-gather = bf16[96,6,128]{2,1,0:T(8,128)(2,1)S(1)} all-gather(bf16[6,6,128]{2,1,0:T(8,128)(2,1)S(1)} %convolution_convert_fusion), channel_id=2, replica_groups=mesh['rep'=16,'fsdp'=32] {'rep'}, dimensions={0}, use_global_device_ids=true | all-gather | bytes 156672 | tf_op jit(solution)/shard_map/all_gather | solution.py:65
  266.1 1.0 fusion.11
  267.1 1.1 convolution_bitcast_fusion.4
  268.2 0.1 reshape.77
  268.3 0.5 convolution_bitcast_fusion.1
  268.8 0.6 multiply_reduce_fusion
  269.5 0.1 tanh_multiply_fusion
  269.6 0.2 copy.36
  269.8 0.2 mul.159
  269.9 1.0 reshape.78
  270.9 0.5 convolution_bitcast_fusion
  271.4 0.5 fusion.3
  272.0 0.2 copy.39
  272.2 0.8 reshape.79
  273.0 1.5 subtract_bitcast_fusion
  274.5 1.5 sub.6
  (9 shorter events, 0.0 us)
Async XLA Ops:
  7.2 1.9 copy-start
  7.2 230.7 %reduce-scatter.2.cloned.1.call-start = ((), (), s32[]{:S(2)}) async-start(), calls=%async_computation.1 | async-start | bytes 3244032 | tf_op jit(solution)/shard_map/reduce_scatter | solution.py:35
  12.6 0.7 copy-start.2
  12.6 26.1 %copy-start.3 = (s32[1,6]{1,0:T(1,128)S(1)}, s32[1,6]{1,0:T(1,128)}, u32[]{:S(2)}) copy-start(s32[1,6]{1,0:T(1,128)} %param.11) | copy-start | bytes 76
  12.6 225.3 %copy-start.1 = (f32[1,192,128]{2,1,0:T(8,128)S(1)}, f32[1,192,128]{2,1,0:T(8,128)}, u32[]{:S(2)}) copy-start(f32[1,192,128]{2,1,0:T(8,128)} %param.8) | copy-start | bytes 294916
Sparse Core Ops, SparseCore 0:
  12.7 225.0 reduce-scatter.1
where the time goes:
time: 283 us
  waiting for transfers between devices  199 us (70%)
  blocking collectives  48.8 us (17%)
  between operations  14.1 us (5%)
  matrix products  9.07 us (3%)
  local copies, waits for them, and re-layouts  7.52 us (3%)
  other arithmetic  4.2 us (1%)
    reduce_scatter x1, waiting for transfers between devices, on_device(): lax.psum_scatter(lax.dot_general(activations, unit_grads, (((0,), (0,)),...  199 us
    all_gather x1, blocking collectives, on_device(): lax.all_gather(block_ids, 'rep', axis=0, tiled=True)  24.6 us
    all_gather x1, blocking collectives, on_device(): lax.all_gather(picked[None], 'rep', axis=0, tiled=True)  24.1 us
  transfers between devices with their start and end apart: 1, of which 1 were waited for; matrix products, arithmetic and copies ran while one was open for 0% of the time, Pallas kernels for 0%

commit v1 on v0

v1 whole, which is shorter than its diff:
```python
import functools

import jax
import jax.numpy as jnp
import ml_dtypes
import numpy as np
from jax import lax
from jax.experimental import pallas as pl
from jax.experimental.pallas import tpu as pltpu
from jax.sharding import PartitionSpec as P

MESH = pl.DeviceIdType.MESH
F32 = jnp.float32
BF16 = jnp.bfloat16

EDGE = 64
NBLK = 32
SLOTS = 6
FW = 128
NX, NY, NREP = 4, 8, 16
TILE_ROWS = 3
ROWS = TILE_ROWS * EDGE
GROUP = NX * ROWS
TOK = 256
H1 = 64
H2 = ROWS - H1
ORDER = (4, 3, 5, 2, 6, 1, 7, 0)
STREAMS = 4


def tables():
    freq = np.arange(EDGE)[:, None].astype(np.float64)
    place = np.arange(EDGE)[None, :].astype(np.float64)
    factor = np.where(freq == 0, np.sqrt(1.0 / EDGE), np.sqrt(2.0 / EDGE))
    table = (factor * np.cos(np.pi * (2.0 * place + 1.0) * freq / (2.0 * EDGE))).astype(np.float32)

    def halves(m):
        hi = m.astype(ml_dtypes.bfloat16)
        lo = (m - hi.astype(np.float32)).astype(ml_dtypes.bfloat16)
        return hi, lo

    both = np.zeros((2 * EDGE, 2 * EDGE), np.float32)
    both[:EDGE, :EDGE] = table
    both[EDGE:, EDGE:] = table
    split = np.concatenate([table[0::2], table[1::2]], axis=0)
    hi, lo = halves(both.T)
    right_fwd = np.concatenate([hi, hi, lo], axis=0)
    hi, lo = halves(both)
    right_inv = np.concatenate([hi, lo, hi], axis=0)
    hi, lo = halves(split)
    left_fwd = np.concatenate([hi, hi, lo], axis=1)
    hi, lo = halves(split.T)
    left_inv = np.concatenate([hi, hi, lo], axis=1)
    return right_fwd, right_inv, left_fwd, left_inv


def dot(a, b):
    return jnp.dot(a, b, preferred_element_type=F32)


def parts_of(v):
    hi = v.astype(BF16)
    lo = (v - hi.astype(F32)).astype(BF16)
    return hi, lo


def kernel(
    a_hbm, u_hbm, mom_hbm, w_hbm, ids_ref, cnt_ref, rf_hbm, ri_hbm, lf_hbm, li_hbm,
    nw_ref, nm_ref,
    a_vm, u_vm, mom_vm, w_vm, rf_vm, ri_vm, lf_vm, li_vm,
    part, y_slots, x_slots, r1, r2, x1_slots, y2_slots,
    code, codes, spread_w, listed, stage, moment_vm,
    load_sem, in_sem,
    y_send, y_recv, x_send, x_recv, x1_send, x1_recv, y2_send, y2_recv,
    c_send, c_recv, g_send, g_recv,
):
    rep = lax.axis_index("rep")
    pos = lax.axis_index("fsdp")
    y = pos // NX
    x = pos % NX

    def at_y(off):
        return ((y + off) % NY) * NX + x

    def at_x(off):
        return y * NX + (x + off) % NX

    def at_rep(off):
        return (rep + off) % NREP

    def load(j):
        t = (y + ORDER[j]) % NY
        cols = pl.ds(pl.multiple_of(t * GROUP, GROUP), GROUP)
        return pltpu.make_async_copy(a_hbm.at[:, cols], a_vm.at[j], load_sem.at[j])

    u_copy = pltpu.make_async_copy(u_hbm, u_vm, in_sem.at[0])
    u_copy.start()
    for j in range(NY):
        load(j).start()
    others = [
        pltpu.make_async_copy(src, dst, in_sem.at[n + 1])
        for n, (src, dst) in enumerate(
            [(mom_hbm, mom_vm), (w_hbm, w_vm), (rf_hbm, rf_vm), (ri_hbm, ri_vm), (lf_hbm, lf_vm), (li_hbm, li_vm)]
        )
    ]
    for copy in others:
        copy.start()

    barrier = pltpu.get_barrier_semaphore()
    for off in range(1, NY):
        pl.semaphore_signal(barrier, inc=1, device_id=(rep, at_y(off)), device_id_type=MESH)
    for off in range(1, NX):
        pl.semaphore_signal(barrier, inc=1, device_id=(rep, at_x(off)), device_id_type=MESH)
    for off in range(1, NREP):
        pl.semaphore_signal(barrier, inc=1, device_id=(at_rep(off), pos), device_id_type=MESH)

    lane8 = lax.broadcasted_iota(jnp.int32, (8, 128), 1)
    row8 = lax.broadcasted_iota(jnp.int32, (8, 128), 0)
    own = lane8 - (rep % 8) * 16
    target = [
        [jnp.where(k < cnt_ref[0, t], ids_ref[0, t, k], -64) for k in range(SLOTS)] for t in range(2 * TILE_ROWS)
    ]
    codes_own = jnp.where((own >= 0) & (own < 16), -64, 0)
    for k in range(SLOTS):
        column = jnp.zeros((8, 128), jnp.int32)
        for t in range(2 * TILE_ROWS):
            column = jnp.where(row8 == t, target[t][k], column)
        codes_own = jnp.where(own == k, column, codes_own)
        codes_own = jnp.where(own == k + SLOTS, column + NBLK, codes_own)
    code[...] = codes_own
    codes[rep] = codes_own

    def remote(src, dst, send, recv, device):
        return pltpu.make_async_remote_copy(
            src_ref=src, dst_ref=dst, send_sem=send, recv_sem=recv, device_id=device, device_id_type=MESH
        )

    y_streams = ((0, 1, 4, 0), (2, -1, 4, 4), (2, 1, 3, 8), (0, -1, 3, 11))

    def y_copy(stream, step):
        xs, way, length, first = y_streams[stream]
        n = first + step
        if step == 0:
            j = ORDER.index((way * length) % NY)
            src = part.at[j, pl.ds(xs, 2), pl.ds(0, H1)]
        else:
            src = y_slots.at[n - 1]
        return remote(src, y_slots.at[n], y_send.at[n], y_recv.at[n], (rep, at_y(way)))

    def y_add(stream, step):
        xs, way, length, first = y_streams[stream]
        y_copy(stream, step).wait_recv()
        j = ORDER.index((way * (length - 1 - step)) % NY)
        n = first + step
        y_slots[n] = (y_slots[n].astype(F32) + part[j, xs : xs + 2, 0:H1].astype(F32)).astype(BF16)

    def x_way(q):
        return 1 if q % 2 == 0 else -1

    def x_copy(q, which):
        way = x_way(q)
        n = 3 * q + which
        rows = pl.ds(2 * q, 2)
        if which == 0:
            src = part.at[rows, (x + 2) % NX, pl.ds(H1, H2)]
        elif which == 1:
            src = x_slots.at[3 * q]
        else:
            src = part.at[rows, (x - way) % NX, pl.ds(H1, H2)]
            way = -way
        return remote(src, x_slots.at[n], x_send.at[n], x_recv.at[n], (rep, at_x(way)))

    def x_mid(q):
        x_copy(q, 0).wait_recv()
        mine = part[2 * q : 2 * q + 2, (x + x_way(q)) % NX, H1:ROWS]
        x_slots[3 * q] = (x_slots[3 * q].astype(F32) + mine.astype(F32)).astype(BF16)
        x_copy(q, 1).start()

    def y2_copy(off):
        j = ORDER.index(off)
        return remote(r2.at[j], y2_slots.at[off - 1], y2_send.at[off - 1], y2_recv.at[off - 1], (rep, at_y(off)))

    def x_last(q):
        x_copy(q, 2).wait_recv()
        x_copy(q, 1).wait_recv()
        mine = part[2 * q : 2 * q + 2, x, H1:ROWS].astype(F32)
        total = mine + x_slots[3 * q + 1].astype(F32) + x_slots[3 * q + 2].astype(F32)
        r2[2 * q : 2 * q + 2] = total.astype(BF16)
        for off in ORDER[2 * q : 2 * q + 2]:
            if off:
                y2_copy(off).start()

    def x1_copy(off):
        return remote(
            r1.at[(x + off) % NX], x1_slots.at[off - 1], x1_send.at[off - 1], x1_recv.at[off - 1], (rep, at_x(off))
        )

    def c_copy(off):
        return remote(code, codes.at[rep], c_send.at[off - 1], c_recv.at[off - 1], (at_rep(off), pos))

    def g_copy(off):
        mine = listed.at[:, rep]
        return remote(mine, mine, g_send.at[off - 1], g_recv.at[off - 1], (at_rep(off), pos))

    pl.semaphore_wait(barrier, NY - 1 + NX - 1 + NREP - 1)
    u_copy.wait()

    for j in range(NY):
        load(j).wait()
        rows = lax.dot_general(a_vm[j], u_vm[...], (((0,), (0,)), ((), ())), preferred_element_type=F32)
        part[j] = rows.astype(BF16).reshape(NX, ROWS, FW)
        if j == 0:
            y_copy(0, 0).start()
            y_copy(1, 0).start()
        if j == 1:
            y_copy(2, 0).start()
        if j == 2:
            y_copy(3, 0).start()
        if j % 2 == 1:
            x_copy(j // 2, 0).start()
            x_copy(j // 2, 2).start()

    for off in range(1, NREP):
        c_copy(off).start()

    def y_round(step):
        for stream in range(4):
            if step < y_streams[stream][2] - 1:
                y_add(stream, step)
                y_copy(stream, step + 1).start()

    y_round(0)
    x_mid(0)
    x_mid(1)
    y_round(1)
    x_mid(2)
    x_mid(3)
    x_last(0)
    x_last(1)
    y_round(2)
    x_last(2)
    x_last(3)

    for half in range(2):
        xs = 2 * half
        total = part[ORDER.index(0), xs : xs + 2, 0:H1].astype(F32)
        for stream in range(4):
            if y_streams[stream][0] == xs:
                last = y_streams[stream][2] - 1
                y_copy(stream, last).wait_recv()
                total += y_slots[y_streams[stream][3] + last].astype(F32)
        r1[xs : xs + 2] = total.astype(BF16)
    for off in range(1, NX):
        x1_copy(off).start()

    for off in range(1, NREP):
        c_copy(off).wait_recv()
    row64 = lax.broadcasted_iota(jnp.int32, (EDGE, 128), 0)
    lane64 = lax.broadcasted_iota(jnp.int32, (EDGE, 128), 1)
    for side in range(NREP // 8):
        tile = codes[8 * side]
        for r in range(1, 8):
            tile += codes[8 * side + r]
        for t in range(2 * TILE_ROWS):
            hit = (tile[t : t + 1] == row64).astype(F32).astype(BF16)
            spread_w[t // 2, EDGE * (t % 2) : EDGE * (t % 2) + EDGE, 128 * side : 128 * side + 128] = hit

    for copy in others:
        copy.wait()

    g1 = r1[x].astype(F32)
    for off in range(1, NX):
        x1_copy(off).wait_recv()
        g1 += x1_slots[off - 1].astype(F32)
    moment_vm[0:H1] = 0.9 * mom_vm[0, 0:H1] + g1
    g2 = r2[ORDER.index(0)].astype(F32)
    for off in range(1, NY):
        y2_copy(off).wait_recv()
        g2 += y2_slots[off - 1].astype(F32)
    moment_vm[H1:ROWS] = 0.9 * mom_vm[0, H1:ROWS] + g2
    moment = moment_vm[...]

    def left(table, v):
        out = []
        for a in range(TILE_ROWS):
            hi, lo = parts_of(v[a * EDGE : a * EDGE + EDGE])
            out.append(dot(table, jnp.concatenate([hi, lo, hi], axis=0)))
        return jnp.concatenate(out, axis=0)

    hi, lo = parts_of(moment)
    coeffs = left(lf_vm[...], dot(jnp.concatenate([hi, lo, hi], axis=1), rf_vm[...])).astype(BF16).astype(F32)
    low_lanes = lane64 < EDGE
    block64 = row64 % NBLK
    keep = []
    stage[...] = jnp.zeros_like(stage)
    for a in range(TILE_ROWS):
        tile = coeffs[a * EDGE : a * EDGE + EDGE]
        live = jnp.zeros((EDGE, 128), F32)
        for k in range(SLOTS):
            chosen = jnp.where(low_lanes, target[2 * a][k], target[2 * a + 1][k]) == block64
            live = jnp.where(chosen, 1.0, live)
            rows = jnp.where(chosen, tile, 0.0)
            stage[a, k : k + 1] = jnp.sum(rows[0:NBLK], axis=0, keepdims=True)
            stage[a, SLOTS + k : SLOTS + k + 1] = jnp.sum(rows[NBLK:EDGE], axis=0, keepdims=True)
        keep.append(tile * live)
    listed[:, rep] = stage[...].astype(BF16)
    for off in range(1, NREP):
        g_copy(off).start()

    removed = jnp.concatenate(keep, axis=0).astype(BF16)
    right_inv = ri_vm[...]
    taken = left(li_vm[...], dot(jnp.concatenate([removed, removed], axis=1), right_inv[0:256]))
    nm_ref[0] = moment - taken

    for off in range(1, NREP):
        g_copy(off).wait_recv()

    summed = []
    for a in range(TILE_ROWS):
        rows = dot(spread_w[a], listed[a].reshape(NREP * 16, 128))
        summed.append(jnp.where(low_lanes, rows[0:EDGE], rows[EDGE : 2 * EDGE]))
    hi, lo = parts_of(jnp.concatenate(summed, axis=0))
    update = left(li_vm[...], dot(jnp.concatenate([hi, hi, lo], axis=1), right_inv))
    lane1 = lax.broadcasted_iota(jnp.int32, (1, 128), 1) < EDGE
    for a in range(TILE_ROWS):
        tile = update[a * EDGE : a * EDGE + EDGE]
        squares = jnp.sum(tile * tile, axis=0, keepdims=True)
        first = jnp.sum(jnp.where(lane1, squares, 0.0), axis=1, keepdims=True)
        second = jnp.sum(jnp.where(lane1, 0.0, squares), axis=1, keepdims=True)
        scale = lax.rsqrt(jnp.where(lane1, first, second) * (1.0 / (EDGE * EDGE)) + 1e-6)
        span = slice(a * EDGE, a * EDGE + EDGE)
        nw_ref[span] = w_vm[span] - 0.25 * jnp.tanh(tile * scale)

    for stream in range(4):
        for step in range(y_streams[stream][2]):
            y_copy(stream, step).wait_send()
    for q in range(STREAMS):
        for which in range(3):
            x_copy(q, which).wait_send()
    for off in range(1, NX):
        x1_copy(off).wait_send()
    for off in range(1, NY):
        y2_copy(off).wait_send()
    for off in range(1, NREP):
        c_copy(off).wait_send()
        g_copy(off).wait_send()


def on_device(activations, unit_grads, momentum, weights, block_ids, block_counts):
    right_fwd, right_inv, left_fwd, left_inv = tables()
    any_spec = pl.BlockSpec(memory_space=pl.ANY)
    smem = pl.BlockSpec(memory_space=pltpu.SMEM)
    vmem = pl.BlockSpec(memory_space=pltpu.VMEM)
    dma = pltpu.SemaphoreType.DMA
    new_weights, new_momentum = pl.pallas_call(
        kernel,
        out_shape=(
            jax.ShapeDtypeStruct(weights.shape, F32),
            jax.ShapeDtypeStruct(momentum.shape, F32),
        ),
        in_specs=[any_spec] * 4 + [smem] * 2 + [any_spec] * 4,
        out_specs=(vmem, vmem),
        scratch_shapes=[
            pltpu.VMEM((NY, TOK, GROUP), BF16),
            pltpu.VMEM((TOK, FW), BF16),
            pltpu.VMEM((1, ROWS, FW), F32),
            pltpu.VMEM((ROWS, FW), F32),
            pltpu.VMEM(right_fwd.shape, BF16),
            pltpu.VMEM(right_inv.shape, BF16),
            pltpu.VMEM(left_fwd.shape, BF16),
            pltpu.VMEM(left_inv.shape, BF16),
            pltpu.VMEM((NY, NX, ROWS, FW), BF16),
            pltpu.VMEM((14, 2, H1, FW), BF16),
            pltpu.VMEM((3 * STREAMS, 2, H2, FW), BF16),
            pltpu.VMEM((NX, H1, FW), BF16),
            pltpu.VMEM((NY, H2, FW), BF16),
            pltpu.VMEM((NX - 1, H1, FW), BF16),
            pltpu.VMEM((NY - 1, H2, FW), BF16),
            pltpu.VMEM((8, 128), jnp.int32),
            pltpu.VMEM((NREP, 8, 128), jnp.int32),
            pltpu.VMEM((TILE_ROWS, 2 * EDGE, NREP * 16), BF16),
            pltpu.VMEM((TILE_ROWS, NREP, 16, 128), BF16),
            pltpu.VMEM((TILE_ROWS, 16, 128), F32),
            pltpu.VMEM((ROWS, FW), F32),
            dma((NY,)),
            dma((7,)),
            dma((14,)), dma((14,)),
            dma((3 * STREAMS,)), dma((3 * STREAMS,)),
            dma((NX - 1,)), dma((NX - 1,)),
            dma((NY - 1,)), dma((NY - 1,)),
            dma((NREP - 1,)), dma((NREP - 1,)),
            dma((NREP - 1,)), dma((NREP - 1,)),
        ],
        compiler_params=pltpu.CompilerParams(
            collective_id=0, has_side_effects=True, vmem_limit_bytes=40 * 1024 * 1024
        ),
    )(activations, unit_grads, momentum, weights, block_ids, block_counts, right_fwd, right_inv, left_fwd, left_inv)
    return new_weights, new_momentum


def solution(mesh):
    placed = (
        P(("rep", "fsdp"), None),
        P(("rep", "fsdp"), None),
        P("rep", "fsdp", None),
        P("fsdp", None),
        P("rep", "fsdp", None),
        P("rep", "fsdp"),
    )
    return jax.shard_map(
        on_device,
        mesh=mesh,
        in_specs=placed,
        out_specs=(P("fsdp", None), P("rep", "fsdp", None)),
        check_vma=False,
    )
```

time: 283 us -> 57.5 us (0.20)
  waiting for transfers between devices: 199 us -> 0 us
  blocking collectives: 48.8 us -> 0 us
  Pallas kernels: 0 us -> 46 us
  between operations: 14.1 us -> 0.65 us
  matrix products: 9.07 us -> 0 us
  other arithmetic: 4.2 us -> 0 us
  local copies, waits for them, and re-layouts: 7.52 us -> 10.4 us
    reduce_scatter x1 -> x0, waiting for transfers between devices: 199 us -> none  [on_device(): lax.psum_scatter(lax.dot_general(activations, unit_grads, (((0,), (0,)),...]
    all_gather x2 -> x0, blocking collectives: 48.8 us -> none  [the longest x1 24.6 us: on_device(): lax.all_gather(block_ids, 'rep', axis=0, tiled=True)]
    pallas_call x0 -> x1, Pallas kernels: none -> 46 us  [on_device(): pl.pallas_call(kernel, out_shape=(jax.ShapeDtypeStruct(weights.shape, F32...]
    dot_general x10 -> x0, matrix products: 9.07 us -> none  [the longest x1 3.53 us: on_device(): lax.dot_general(activations, unit_grads, (((0,), (0,)), ((), ())), prefer...]
    unnamed x9 -> x21, local copies, waits for them, and re-layouts: 2.51 us -> 10.4 us
    reshape x5 -> x0, local copies, waits for them, and re-layouts: 3.04 us -> none  [the longest x1 1.01 us: on_device(): forward_tiles(moment.reshape(rows_a, EDGE, cols_b, EDGE), table)]
  transfers between devices with their start and end apart: 1 -> 0, of which waited for: 1 -> 0; matrix products, arithmetic and copies ran while one was open for 0% -> 0% of each run, Pallas kernels for 0% -> 0%
where the time goes in v1:
time: 57.5 us; the launch traced here: 57 us
  Pallas kernels  46 us (80%)
  local copies, waits for them, and re-layouts  10.4 us (18%)
  between operations  0.65 us (1%)
    pallas_call x1, Pallas kernels, on_device(): pl.pallas_call(kernel, out_shape=(jax.ShapeDtypeStruct(weights.shape, F32...  46 us
    unnamed x21, local copies, waits for them, and re-layouts  10.4 us

profile of v1, /device:TPU:1, one launch (start us, length us, event | category | flops | bytes accessed | tf_op | source)
XLA Modules:
  0.0 57.0 jit_solution(12175786165670671641)
XLA Ops:
  0.6 0.7 %copy.12.ids_ref = s32[1,6,6]{2,1,0:T(8,128)S(1)} copy(s32[1,6,6]{2,0,1:T(1,128)} %param.14) | data formatting | bytes 288 | tf_op args[4]
  1.3 0.0 copy-start
  1.3 1.9 %copy-done = bf16[256,6144]{1,0:T(8,128)(2,1)S(1)} copy-done((bf16[256,6144]{1,0:T(8,128)(2,1)S(1)}, bf16[256,6144]{1,0:T(8,128)(2,1)}, u32[]{:S(2)}) %copy-start) | copy-done | bytes 3145752
  3.2 0.0 copy-start.1
  3.2 0.9 %copy-done.1 = f32[1,192,128]{2,1,0:T(8,128)S(1)} copy-done((f32[1,192,128]{2,1,0:T(8,128)S(1)}, f32[1,192,128]{2,1,0:T(8,128)}, u32[]{:S(2)}) %copy-start.1) | copy-done | bytes 98328
  4.1 0.0 copy-start.2
  4.1 0.9 %copy-done.2 = f32[192,128]{1,0:T(8,128)S(1)} copy-done((f32[192,128]{1,0:T(8,128)S(1)}, f32[192,128]{1,0:T(8,128)}, u32[]{:S(2)}) %copy-start.2) | copy-done | bytes 98328
  5.0 0.0 copy-start.3
  5.0 0.9 %copy-done.3 = bf16[384,128]{1,0:T(8,128)(2,1)S(1)} copy-done((bf16[384,128]{1,0:T(8,128)(2,1)S(1)}, bf16[384,128]{1,0:T(8,128)(2,1)}, u32[]{:S(2)}) %copy-start.3) | copy-done | bytes 98328
  5.9 0.0 copy-start.4
  5.9 0.9 %copy-done.4 = bf16[384,128]{1,0:T(8,128)(2,1)S(1)} copy-done((bf16[384,128]{1,0:T(8,128)(2,1)S(1)}, bf16[384,128]{1,0:T(8,128)(2,1)}, u32[]{:S(2)}) %copy-start.4) | copy-done | bytes 98328
  6.8 0.0 copy-start.5
  6.8 0.8 %copy-done.5 = bf16[256,128]{1,0:T(8,128)(2,1)S(1)} copy-done((bf16[256,128]{1,0:T(8,128)(2,1)S(1)}, bf16[256,128]{1,0:T(8,128)(2,1)}, u32[]{:S(2)}) %copy-start.5) | copy-done | bytes 65560
  7.6 0.0 copy-start.6
  7.6 0.8 %copy-done.6 = bf16[64,192]{1,0:T(8,128)(2,1)S(1)} copy-done((bf16[64,192]{1,0:T(8,128)(2,1)S(1)}, bf16[64,192]{1,0:T(8,128)(2,1)}, u32[]{:S(2)}) %copy-start.6) | copy-done | bytes 24600
  8.4 0.0 copy-start.7
  8.4 0.8 %copy-done.7 = bf16[64,192]{1,0:T(8,128)(2,1)S(1)} copy-done((bf16[64,192]{1,0:T(8,128)(2,1)S(1)}, bf16[64,192]{1,0:T(8,128)(2,1)}, u32[]{:S(2)}) %copy-start.7) | copy-done | bytes 24600
  9.1 0.0 copy-start.8
  9.1 0.7 %copy-done.8 = s32[1,6]{1,0:T(1,128)S(1)} copy-done((s32[1,6]{1,0:T(1,128)S(1)}, s32[1,6]{1,0:T(1,128)}, u32[]{:S(2)}) %copy-start.8) | copy-done | bytes 48
  9.8 46.0 %shard_map.113 = (f32[192,128]{1,0:T(8,128)S(1)}, f32[1,192,128]{2,1,0:T(8,128)S(1)}) custom-call(bf16[256,6144]{1,0:T(8,128)(2,1)S(1)} %copy-done, bf16[256,128]{1,0:T(8,128)(2,1)S(1)} %copy-done.5, f32[1,192,128]{2,1,0:T(8,128)S(1)} %copy-done.1, f32[192,128]{1,0:T(8,128)S(1)} %copy-done.2, s32[1,6,6]{2,1,0:T(8,128)S(1)} %copy.12.ids_ref, ...), custom_call_target="tpu_custom_call" | custom-call | tf_op jit(solution)/shard_map/pallas_call | solution.py:355
  55.8 0.6 %copy.15 = f32[192,128]{1,0:T(8,128)} copy(f32[192,128]{1,0:T(8,128)S(1)} %get-tuple-element.4) | data formatting | bytes 196608
  56.4 0.6 %copy.16 = f32[1,192,128]{2,1,0:T(8,128)} copy(f32[1,192,128]{2,1,0:T(8,128)S(1)} %get-tuple-element.5) | data formatting | bytes 196608
Async XLA Ops:
  1.3 1.9 %copy-start = (bf16[256,6144]{1,0:T(8,128)(2,1)S(1)}, bf16[256,6144]{1,0:T(8,128)(2,1)}, u32[]{:S(2)}) copy-start(bf16[256,6144]{1,0:T(8,128)(2,1)} %a_hbm.1) | copy-start | bytes 9437188
  3.2 0.9 %copy-start.1 = (f32[1,192,128]{2,1,0:T(8,128)S(1)}, f32[1,192,128]{2,1,0:T(8,128)}, u32[]{:S(2)}) copy-start(f32[1,192,128]{2,1,0:T(8,128)} %mom_hbm.1) | copy-start | bytes 294916
  4.1 0.9 %copy-start.2 = (f32[192,128]{1,0:T(8,128)S(1)}, f32[192,128]{1,0:T(8,128)}, u32[]{:S(2)}) copy-start(f32[192,128]{1,0:T(8,128)} %w_hbm.1) | copy-start | bytes 294916
  5.0 0.9 %copy-start.3 = (bf16[384,128]{1,0:T(8,128)(2,1)S(1)}, bf16[384,128]{1,0:T(8,128)(2,1)}, u32[]{:S(2)}) copy-start(bf16[384,128]{1,0:T(8,128)(2,1)} %constant.9.clone.ri_hbm) | copy-start | bytes 294916
  5.9 0.9 %copy-start.4 = (bf16[384,128]{1,0:T(8,128)(2,1)S(1)}, bf16[384,128]{1,0:T(8,128)(2,1)}, u32[]{:S(2)}) copy-start(bf16[384,128]{1,0:T(8,128)(2,1)} %constant.8.clone.rf_hbm) | copy-start | bytes 294916
  6.8 0.8 %copy-start.5 = (bf16[256,128]{1,0:T(8,128)(2,1)S(1)}, bf16[256,128]{1,0:T(8,128)(2,1)}, u32[]{:S(2)}) copy-start(bf16[256,128]{1,0:T(8,128)(2,1)} %u_hbm.1) | copy-start | bytes 196612
  7.6 0.8 %copy-start.6 = (bf16[64,192]{1,0:T(8,128)(2,1)S(1)}, bf16[64,192]{1,0:T(8,128)(2,1)}, u32[]{:S(2)}) copy-start(bf16[64,192]{1,0:T(8,128)(2,1)} %constant.11.clone.li_hbm) | copy-start | bytes 73732
  8.4 0.8 %copy-start.7 = (bf16[64,192]{1,0:T(8,128)(2,1)S(1)}, bf16[64,192]{1,0:T(8,128)(2,1)}, u32[]{:S(2)}) copy-start(bf16[64,192]{1,0:T(8,128)(2,1)} %constant.10.clone.lf_hbm) | copy-start | bytes 73732
  9.1 0.7 %copy-start.8 = (s32[1,6]{1,0:T(1,128)S(1)}, s32[1,6]{1,0:T(1,128)}, u32[]{:S(2)}) copy-start(s32[1,6]{1,0:T(1,128)} %cnt_ref.1) | copy-start | bytes 76

commit v2 on v1

--- a/solution.py
+++ b/solution.py
@@ -22,7 +22,7 @@
 ROWS = TILE_ROWS * EDGE
 GROUP = NX * ROWS
 TOK = 256
-H1 = 64
+H1 = 96
 H2 = ROWS - H1
 ORDER = (4, 3, 5, 2, 6, 1, 7, 0)
 STREAMS = 4
@@ -65,10 +65,10 @@
 
 
 def kernel(
-    a_hbm, u_hbm, mom_hbm, w_hbm, ids_ref, cnt_ref, rf_hbm, ri_hbm, lf_hbm, li_hbm,
+    a_hbm, u_hbm, mom_hbm, w_hbm, ids_hbm, cnt_hbm, rf_hbm, ri_hbm, lf_hbm, li_hbm,
     nw_ref, nm_ref,
     a_vm, u_vm, mom_vm, w_vm, rf_vm, ri_vm, lf_vm, li_vm,
-    part, y_slots, x_slots, r1, r2, x1_slots, y2_slots,
+    ids_ref, cnt_ref, part, y_slots, x_slots, r1, r2, x1_slots, y2_slots,
     code, codes, spread_w, listed, stage, moment_vm,
     load_sem, in_sem,
     y_send, y_recv, x_send, x_recv, x1_send, x1_recv, y2_send, y2_recv,
@@ -94,16 +94,18 @@
         return pltpu.make_async_copy(a_hbm.at[:, cols], a_vm.at[j], load_sem.at[j])
 
     u_copy = pltpu.make_async_copy(u_hbm, u_vm, in_sem.at[0])
+    others = [
+        pltpu.make_async_copy(src, dst, in_sem.at[n + 1])
+        for n, (src, dst) in enumerate(
+            [(ids_hbm, ids_ref), (cnt_hbm, cnt_ref), (mom_hbm, mom_vm), (w_hbm, w_vm), (rf_hbm, rf_vm), (ri_hbm, ri_vm), (lf_hbm, lf_vm), (li_hbm, li_vm)]
+        )
+    ]
+    for copy in others[0:2]:
+        copy.start()
     u_copy.start()
     for j in range(NY):
         load(j).start()
-    others = [
-        pltpu.make_async_copy(src, dst, in_sem.at[n + 1])
-        for n, (src, dst) in enumerate(
-            [(mom_hbm, mom_vm), (w_hbm, w_vm), (rf_hbm, rf_vm), (ri_hbm, ri_vm), (lf_hbm, lf_vm), (li_hbm, li_vm)]
-        )
-    ]
-    for copy in others:
+    for copy in others[2:]:
         copy.start()
 
     barrier = pltpu.get_barrier_semaphore()
@@ -114,11 +116,13 @@
     for off in range(1, NREP):
         pl.semaphore_signal(barrier, inc=1, device_id=(at_rep(off), pos), device_id_type=MESH)
 
+    for copy in others[0:2]:
+        copy.wait()
     lane8 = lax.broadcasted_iota(jnp.int32, (8, 128), 1)
     row8 = lax.broadcasted_iota(jnp.int32, (8, 128), 0)
     own = lane8 - (rep % 8) * 16
     target = [
-        [jnp.where(k < cnt_ref[0, t], ids_ref[0, t, k], -64) for k in range(SLOTS)] for t in range(2 * TILE_ROWS)
+        [jnp.where(k < cnt_ref[0, t], ids_ref[t, 0, k], -64) for k in range(SLOTS)] for t in range(2 * TILE_ROWS)
     ]
     codes_own = jnp.where((own >= 0) & (own < 16), -64, 0)
     for k in range(SLOTS):
@@ -130,10 +134,22 @@
     code[...] = codes_own
     codes[rep] = codes_own
 
-    def remote(src, dst, send, recv, device):
-        return pltpu.make_async_remote_copy(
-            src_ref=src, dst_ref=dst, send_sem=send, recv_sem=recv, device_id=device, device_id_type=MESH
-        )
+    started = []
+
+    class Sent:
+        def __init__(self, src, dst, send, recv, device):
+            self.copy = pltpu.make_async_remote_copy(
+                src_ref=src, dst_ref=dst, send_sem=send, recv_sem=recv, device_id=device, device_id_type=MESH
+            )
+
+        def start(self):
+            self.copy.start()
+            started.append(self.copy)
+
+        def wait_recv(self):
+            self.copy.wait_recv()
+
+    remote = Sent
 
     y_streams = ((0, 1, 4, 0), (2, -1, 4, 4), (2, 1, 3, 8), (0, -1, 3, 11))
 
@@ -265,7 +281,7 @@
             hit = (tile[t : t + 1] == row64).astype(F32).astype(BF16)
             spread_w[t // 2, EDGE * (t % 2) : EDGE * (t % 2) + EDGE, 128 * side : 128 * side + 128] = hit
 
-    for copy in others:
+    for copy in others[2:]:
         copy.wait()
 
     g1 = r1[x].astype(F32)
@@ -331,25 +347,13 @@
         span = slice(a * EDGE, a * EDGE + EDGE)
         nw_ref[span] = w_vm[span] - 0.25 * jnp.tanh(tile * scale)
 
-    for stream in range(4):
-        for step in range(y_streams[stream][2]):
-            y_copy(stream, step).wait_send()
-    for q in range(STREAMS):
-        for which in range(3):
-            x_copy(q, which).wait_send()
-    for off in range(1, NX):
-        x1_copy(off).wait_send()
-    for off in range(1, NY):
-        y2_copy(off).wait_send()
-    for off in range(1, NREP):
-        c_copy(off).wait_send()
-        g_copy(off).wait_send()
+    for copy in started:
+        copy.wait_send()
 
 
 def on_device(activations, unit_grads, momentum, weights, block_ids, block_counts):
     right_fwd, right_inv, left_fwd, left_inv = tables()
-    any_spec = pl.BlockSpec(memory_space=pl.ANY)
-    smem = pl.BlockSpec(memory_space=pltpu.SMEM)
+    hbm = pl.BlockSpec(memory_space=pltpu.HBM)
     vmem = pl.BlockSpec(memory_space=pltpu.VMEM)
     dma = pltpu.SemaphoreType.DMA
     new_weights, new_momentum = pl.pallas_call(
@@ -358,7 +362,7 @@
             jax.ShapeDtypeStruct(weights.shape, F32),
             jax.ShapeDtypeStruct(momentum.shape, F32),
         ),
-        in_specs=[any_spec] * 4 + [smem] * 2 + [any_spec] * 4,
+        in_specs=[hbm] * 10,
         out_specs=(vmem, vmem),
         scratch_shapes=[
             pltpu.VMEM((NY, TOK, GROUP), BF16),
@@ -369,6 +373,8 @@
             pltpu.VMEM(right_inv.shape, BF16),
             pltpu.VMEM(left_fwd.shape, BF16),
             pltpu.VMEM(left_inv.shape, BF16),
+            pltpu.SMEM((2 * TILE_ROWS, 1, SLOTS), jnp.int32),
+            pltpu.SMEM((1, 2 * TILE_ROWS), jnp.int32),
             pltpu.VMEM((NY, NX, ROWS, FW), BF16),
             pltpu.VMEM((14, 2, H1, FW), BF16),
             pltpu.VMEM((3 * STREAMS, 2, H2, FW), BF16),
@@ -383,7 +389,7 @@
             pltpu.VMEM((TILE_ROWS, 16, 128), F32),
             pltpu.VMEM((ROWS, FW), F32),
             dma((NY,)),
-            dma((7,)),
+            dma((9,)),
             dma((14,)), dma((14,)),
             dma((3 * STREAMS,)), dma((3 * STREAMS,)),
             dma((NX - 1,)), dma((NX - 1,)),
@@ -392,9 +398,9 @@
             dma((NREP - 1,)), dma((NREP - 1,)),
         ],
         compiler_params=pltpu.CompilerParams(
-            collective_id=0, has_side_effects=True, vmem_limit_bytes=40 * 1024 * 1024
+            collective_id=0, has_side_effects=True, vmem_limit_bytes=60 * 1024 * 1024
         ),
-    )(activations, unit_grads, momentum, weights, block_ids, block_counts, right_fwd, right_inv, left_fwd, left_inv)
+    )(activations, unit_grads, momentum, weights, jnp.transpose(block_ids, (1, 0, 2)), block_counts, right_fwd, right_inv, left_fwd, left_inv)
     return new_weights, new_momentum
 
 

time: 57.5 us -> 48.1 us (0.84)
  local copies, waits for them, and re-layouts: 10.4 us -> 3.08 us
  Pallas kernels: 46 us -> 44.2 us
    unnamed x21 -> x2, local copies, waits for them, and re-layouts: 10.4 us -> 3.08 us
    pallas_call x1, Pallas kernels: 46 us -> 44.2 us  [on_device(): pl.pallas_call(kernel, out_shape=(jax.ShapeDtypeStruct(weights.shape, F32...]
where the time goes in v2:
time: 48.1 us; the launch traced here: 47.9 us
  Pallas kernels  44.2 us (92%)
  local copies, waits for them, and re-layouts  3.08 us (6%)
  between operations  0.64 us (1%)
    pallas_call x1, Pallas kernels, on_device(): pl.pallas_call(kernel, out_shape=(jax.ShapeDtypeStruct(weights.shape, F32...  44.2 us
    unnamed x2, local copies, waits for them, and re-layouts  3.08 us

profile of v2, /device:TPU:1, one launch (start us, length us, event | category | flops | bytes accessed | tf_op | source)
XLA Modules:
  0.0 47.9 jit_solution(14571316094966710160)
XLA Ops:
  0.6 44.2 %shard_map.113 = (f32[192,128]{1,0:T(8,128)}, f32[1,192,128]{2,1,0:T(8,128)}) custom-call(bf16[256,6144]{1,0:T(8,128)(2,1)} %a_hbm.1, bf16[256,128]{1,0:T(8,128)(2,1)} %u_hbm.1, f32[1,192,128]{2,1,0:T(8,128)} %mom_hbm.1, f32[192,128]{1,0:T(8,128)} %w_hbm.1, s32[6,1,6]{2,1,0:T(1,128)} %bitcast.1, s32[1,6]{1,0:T(1,128)} %cnt_hbm.1, ...), custom_call_target="tpu_custom_call" | custom-call | tf_op jit(solution)/shard_map/pallas_call | solution.py:359
  44.8 1.5 %copy.14 = f32[192,128]{1,0:T(8,128)} copy(f32[192,128]{1,0:T(8,128)} %get-tuple-element.4) | data formatting | bytes 196608
  46.4 1.5 %copy.15 = f32[1,192,128]{2,1,0:T(8,128)} copy(f32[1,192,128]{2,1,0:T(8,128)} %get-tuple-element.5) | data formatting | bytes 196608

commit v3 on v2

--- a/solution.py
+++ b/solution.py
@@ -22,7 +22,7 @@
 ROWS = TILE_ROWS * EDGE
 GROUP = NX * ROWS
 TOK = 256
-H1 = 96
+H1 = 64
 H2 = ROWS - H1
 ORDER = (4, 3, 5, 2, 6, 1, 7, 0)
 STREAMS = 4
@@ -66,7 +66,7 @@
 
 def kernel(
     a_hbm, u_hbm, mom_hbm, w_hbm, ids_hbm, cnt_hbm, rf_hbm, ri_hbm, lf_hbm, li_hbm,
-    nw_ref, nm_ref,
+    out_ref,
     a_vm, u_vm, mom_vm, w_vm, rf_vm, ri_vm, lf_vm, li_vm,
     ids_ref, cnt_ref, part, y_slots, x_slots, r1, r2, x1_slots, y2_slots,
     code, codes, spread_w, listed, stage, moment_vm,
@@ -151,24 +151,31 @@
 
     remote = Sent
 
-    y_streams = ((0, 1, 4, 0), (2, -1, 4, 4), (2, 1, 3, 8), (0, -1, 3, 11))
-
-    def y_copy(stream, step):
-        xs, way, length, first = y_streams[stream]
-        n = first + step
-        if step == 0:
-            j = ORDER.index((way * length) % NY)
-            src = part.at[j, pl.ds(xs, 2), pl.ds(0, H1)]
+    y_moves = ((3, 0, NX, 1), (5, 0, NX, -1), (4, 0, 2, 2), (4, 2, 2, -2), (2, 0, NX, 2), (6, 0, NX, -2), (1, 0, NX, 1), (7, 0, NX, -1))
+
+    def y_slot(n):
+        return y_slots.at[n, pl.ds(0, y_moves[n][2])]
+
+    def y_copy(n):
+        off, first, count, hops = y_moves[n]
+        if n == 4 or n == 5:
+            src = y_slot(n - 4)
         else:
-            src = y_slots.at[n - 1]
-        return remote(src, y_slots.at[n], y_send.at[n], y_recv.at[n], (rep, at_y(way)))
-
-    def y_add(stream, step):
-        xs, way, length, first = y_streams[stream]
-        y_copy(stream, step).wait_recv()
-        j = ORDER.index((way * (length - 1 - step)) % NY)
-        n = first + step
-        y_slots[n] = (y_slots[n].astype(F32) + part[j, xs : xs + 2, 0:H1].astype(F32)).astype(BF16)
+            src = part.at[ORDER.index(off), pl.ds(first, count), pl.ds(0, H1)]
+        return remote(src, y_slot(n), y_send.at[n], y_recv.at[n], (rep, at_y(hops)))
+
+    def y_mid(side):
+        first = y_moves[2 + side][1]
+        y_copy(side).wait_recv()
+        y_copy(2 + side).wait_recv()
+        mine = part.at[ORDER.index(y_moves[4 + side][0])]
+        near = slice(first, first + 2)
+        rest = slice(2 - first, 4 - first)
+        total = y_slots[side, near].astype(F32) + y_slots[2 + side, 0:2].astype(F32) + mine[near, 0:H1].astype(F32)
+        y_slots[side, near] = total.astype(BF16)
+        total = y_slots[side, rest].astype(F32) + mine[rest, 0:H1].astype(F32)
+        y_slots[side, rest] = total.astype(BF16)
+        y_copy(4 + side).start()
 
     def x_way(q):
         return 1 if q % 2 == 0 else -1
@@ -218,56 +225,49 @@
         mine = listed.at[:, rep]
         return remote(mine, mine, g_send.at[off - 1], g_recv.at[off - 1], (at_rep(off), pos))
 
-    pl.semaphore_wait(barrier, NY - 1 + NX - 1 + NREP - 1)
     u_copy.wait()
-
-    for j in range(NY):
-        load(j).wait()
-        rows = lax.dot_general(a_vm[j], u_vm[...], (((0,), (0,)), ((), ())), preferred_element_type=F32)
-        part[j] = rows.astype(BF16).reshape(NX, ROWS, FW)
-        if j == 0:
-            y_copy(0, 0).start()
-            y_copy(1, 0).start()
-        if j == 1:
-            y_copy(2, 0).start()
-        if j == 2:
-            y_copy(3, 0).start()
-        if j % 2 == 1:
-            x_copy(j // 2, 0).start()
-            x_copy(j // 2, 2).start()
-
-    for off in range(1, NREP):
-        c_copy(off).start()
-
-    def y_round(step):
-        for stream in range(4):
-            if step < y_streams[stream][2] - 1:
-                y_add(stream, step)
-                y_copy(stream, step + 1).start()
-
-    y_round(0)
+    grads = u_vm[...].T
+
+    for q in range(STREAMS):
+        load(2 * q).wait()
+        load(2 * q + 1).wait()
+        for j in range(2 * q, 2 * q + 2):
+            columns = jnp.dot(grads, a_vm[j], preferred_element_type=F32).astype(BF16)
+            part[j] = columns.T.reshape(NX, ROWS, FW)
+        if q == 0:
+            pl.semaphore_wait(barrier, NY - 1 + NX - 1 + NREP - 1)
+            y_copy(0).start()
+            y_copy(2).start()
+            y_copy(3).start()
+        if q == 1:
+            y_copy(1).start()
+        if q == 2:
+            y_copy(6).start()
+        if q == 3:
+            y_copy(7).start()
+        x_copy(q, 0).start()
+        x_copy(q, 2).start()
+
+    y_mid(0)
+    y_mid(1)
     x_mid(0)
     x_mid(1)
-    y_round(1)
     x_mid(2)
     x_mid(3)
     x_last(0)
     x_last(1)
-    y_round(2)
+    for off in range(1, NREP):
+        c_copy(off).start()
+
+    total = part[ORDER.index(0), :, 0:H1].astype(F32)
+    for n in (6, 7, 4, 5):
+        y_copy(n).wait_recv()
+        total += y_slots[n].astype(F32)
+    r1[...] = total.astype(BF16)
+    for off in range(1, NX):
+        x1_copy(off).start()
     x_last(2)
     x_last(3)
-
-    for half in range(2):
-        xs = 2 * half
-        total = part[ORDER.index(0), xs : xs + 2, 0:H1].astype(F32)
-        for stream in range(4):
-            if y_streams[stream][0] == xs:
-                last = y_streams[stream][2] - 1
-                y_copy(stream, last).wait_recv()
-                total += y_slots[y_streams[stream][3] + last].astype(F32)
-        r1[xs : xs + 2] = total.astype(BF16)
-    for off in range(1, NX):
-        x1_copy(off).start()
 
     for off in range(1, NREP):
         c_copy(off).wait_recv()
@@ -326,8 +326,10 @@
     removed = jnp.concatenate(keep, axis=0).astype(BF16)
     right_inv = ri_vm[...]
     taken = left(li_vm[...], dot(jnp.concatenate([removed, removed], axis=1), right_inv[0:256]))
-    nm_ref[0] = moment - taken
-
+    out_ref[1] = moment - taken
+
+    for copy in started:
+        copy.wait_send()
     for off in range(1, NREP):
         g_copy(off).wait_recv()
 
@@ -345,25 +347,18 @@
         second = jnp.sum(jnp.where(lane1, 0.0, squares), axis=1, keepdims=True)
         scale = lax.rsqrt(jnp.where(lane1, first, second) * (1.0 / (EDGE * EDGE)) + 1e-6)
         span = slice(a * EDGE, a * EDGE + EDGE)
-        nw_ref[span] = w_vm[span] - 0.25 * jnp.tanh(tile * scale)
-
-    for copy in started:
-        copy.wait_send()
+        out_ref[0, span] = w_vm[span] - 0.25 * jnp.tanh(tile * scale)
 
 
 def on_device(activations, unit_grads, momentum, weights, block_ids, block_counts):
     right_fwd, right_inv, left_fwd, left_inv = tables()
     hbm = pl.BlockSpec(memory_space=pltpu.HBM)
-    vmem = pl.BlockSpec(memory_space=pltpu.VMEM)
     dma = pltpu.SemaphoreType.DMA
-    new_weights, new_momentum = pl.pallas_call(
+    both = pl.pallas_call(
         kernel,
-        out_shape=(
-            jax.ShapeDtypeStruct(weights.shape, F32),
-            jax.ShapeDtypeStruct(momentum.shape, F32),
-        ),
+        out_shape=pltpu.VMEM((2, ROWS, FW), F32),
         in_specs=[hbm] * 10,
-        out_specs=(vmem, vmem),
+        out_specs=pl.BlockSpec(memory_space=pltpu.VMEM),
         scratch_shapes=[
             pltpu.VMEM((NY, TOK, GROUP), BF16),
             pltpu.VMEM((TOK, FW), BF16),
@@ -376,7 +371,7 @@
             pltpu.SMEM((2 * TILE_ROWS, 1, SLOTS), jnp.int32),
             pltpu.SMEM((1, 2 * TILE_ROWS), jnp.int32),
             pltpu.VMEM((NY, NX, ROWS, FW), BF16),
-            pltpu.VMEM((14, 2, H1, FW), BF16),
+            pltpu.VMEM((8, NX, H1, FW), BF16),
             pltpu.VMEM((3 * STREAMS, 2, H2, FW), BF16),
             pltpu.VMEM((NX, H1, FW), BF16),
             pltpu.VMEM((NY, H2, FW), BF16),
@@ -390,7 +385,7 @@
             pltpu.VMEM((ROWS, FW), F32),
             dma((NY,)),
             dma((9,)),
-            dma((14,)), dma((14,)),
+            dma((8,)), dma((8,)),
             dma((3 * STREAMS,)), dma((3 * STREAMS,)),
             dma((NX - 1,)), dma((NX - 1,)),
             dma((NY - 1,)), dma((NY - 1,)),
@@ -401,7 +396,7 @@
             collective_id=0, has_side_effects=True, vmem_limit_bytes=60 * 1024 * 1024
         ),
     )(activations, unit_grads, momentum, weights, jnp.transpose(block_ids, (1, 0, 2)), block_counts, right_fwd, right_inv, left_fwd, left_inv)
-    return new_weights, new_momentum
+    return both[0], both[1:2]
 
 
 def solution(mesh):

time: 48.1 us -> 41.5 us (0.86)
  Pallas kernels: 44.2 us -> 40.1 us
  local copies, waits for them, and re-layouts: 3.08 us -> 0.69 us
    pallas_call x1, Pallas kernels: 44.2 us -> 40.1 us  [on_device(): pl.pallas_call(kernel, out_shape=pltpu.VMEM((2, ROWS, FW), F32), in_specs...]
    unnamed x2 -> x0, local copies, waits for them, and re-layouts: 3.08 us -> none
    slice x0 -> x1, local copies, waits for them, and re-layouts: none -> 0.69 us  [on_device(): return (both[0], both[1:2])]
where the time goes in v3:
time: 41.5 us; the launch traced here: 41.4 us
  Pallas kernels  40.1 us (97%)
  local copies, waits for them, and re-layouts  0.69 us (2%)
  between operations  0.64 us (2%)
    pallas_call x1, Pallas kernels, on_device(): pl.pallas_call(kernel, out_shape=pltpu.VMEM((2, ROWS, FW), F32), in_specs...  40.1 us

profile of v3, /device:TPU:1, one launch (start us, length us, event | category | flops | bytes accessed | tf_op | source)
XLA Modules:
  0.0 41.4 jit_solution(13804685926842553332)
XLA Ops:
  0.6 40.1 %shard_map.113 = f32[2,192,128]{2,1,0:T(8,128)S(1)} custom-call(bf16[256,6144]{1,0:T(8,128)(2,1)} %a_hbm.1, bf16[256,128]{1,0:T(8,128)(2,1)} %u_hbm.1, f32[1,192,128]{2,1,0:T(8,128)} %mom_hbm.1, f32[192,128]{1,0:T(8,128)} %w_hbm.1, s32[6,1,6]{2,1,0:T(1,128)} %bitcast.3, s32[1,6]{1,0:T(1,128)} %cnt_hbm.1, bf16[384,128]{1,0:T(8,128)(2,1)} %constant.8.clone.rf_hbm, ...), custom_call_target="tpu_custom_call" | custom-call | tf_op jit(solution)/shard_map/pallas_call | solution.py:357
  40.7 0.7 %fusion = (f32[1,192,128]{2,1,0:T(8,128)}, f32[192,128]{1,0:T(8,128)}) fusion(f32[2,192,128]{2,1,0:T(8,128)S(1)} %shard_map.113), kind=kLoop, calls=%fused_computation.1 | loop fusion | bytes 393216 | tf_op jit(solution)/shard_map/slice | solution.py:399

commit v4 on v3

--- a/solution.py
+++ b/solution.py
@@ -26,6 +26,8 @@
 H2 = ROWS - H1
 ORDER = (4, 3, 5, 2, 6, 1, 7, 0)
 STREAMS = 4
+REPLICAS = (8, 7, 9, 6, 10, 5, 11, 4, 12, 3, 13, 2, 14, 1, 15)
+PIECES = (slice(0, 1), slice(1, 3))
 
 
 def tables():
@@ -69,7 +71,7 @@
     out_ref,
     a_vm, u_vm, mom_vm, w_vm, rf_vm, ri_vm, lf_vm, li_vm,
     ids_ref, cnt_ref, part, y_slots, x_slots, r1, r2, x1_slots, y2_slots,
-    code, codes, spread_w, listed, stage, moment_vm,
+    code, codes, spread_w, listed, stage,
     load_sem, in_sem,
     y_send, y_recv, x_send, x_recv, x1_send, x1_recv, y2_send, y2_recv,
     c_send, c_recv, g_send, g_recv,
@@ -87,6 +89,12 @@
 
     def at_rep(off):
         return (rep + off) % NREP
+
+    barrier = pltpu.get_barrier_semaphore()
+    for off in range(1, NY):
+        pl.semaphore_signal(barrier, inc=1, device_id=(rep, at_y(off)), device_id_type=MESH)
+    for off in range(1, NX):
+        pl.semaphore_signal(barrier, inc=1, device_id=(rep, at_x(off)), device_id_type=MESH)
 
     def load(j):
         t = (y + ORDER[j]) % NY
@@ -103,36 +111,16 @@
     for copy in others[0:2]:
         copy.start()
     u_copy.start()
-    for j in range(NY):
+    for j in range(2):
+        load(j).start()
+
+    for off in range(1, NREP):
+        pl.semaphore_signal(barrier, inc=1, device_id=(at_rep(off), pos), device_id_type=MESH)
+
+    for j in range(2, NY):
         load(j).start()
     for copy in others[2:]:
         copy.start()
-
-    barrier = pltpu.get_barrier_semaphore()
-    for off in range(1, NY):
-        pl.semaphore_signal(barrier, inc=1, device_id=(rep, at_y(off)), device_id_type=MESH)
-    for off in range(1, NX):
-        pl.semaphore_signal(barrier, inc=1, device_id=(rep, at_x(off)), device_id_type=MESH)
-    for off in range(1, NREP):
-        pl.semaphore_signal(barrier, inc=1, device_id=(at_rep(off), pos), device_id_type=MESH)
-
-    for copy in others[0:2]:
-        copy.wait()
-    lane8 = lax.broadcasted_iota(jnp.int32, (8, 128), 1)
-    row8 = lax.broadcasted_iota(jnp.int32, (8, 128), 0)
-    own = lane8 - (rep % 8) * 16
-    target = [
-        [jnp.where(k < cnt_ref[0, t], ids_ref[t, 0, k], -64) for k in range(SLOTS)] for t in range(2 * TILE_ROWS)
-    ]
-    codes_own = jnp.where((own >= 0) & (own < 16), -64, 0)
-    for k in range(SLOTS):
-        column = jnp.zeros((8, 128), jnp.int32)
-        for t in range(2 * TILE_ROWS):
-            column = jnp.where(row8 == t, target[t][k], column)
-        codes_own = jnp.where(own == k, column, codes_own)
-        codes_own = jnp.where(own == k + SLOTS, column + NBLK, codes_own)
-    code[...] = codes_own
-    codes[rep] = codes_own
 
     started = []
 
@@ -221,9 +209,10 @@
     def c_copy(off):
         return remote(code, codes.at[rep], c_send.at[off - 1], c_recv.at[off - 1], (at_rep(off), pos))
 
-    def g_copy(off):
-        mine = listed.at[:, rep]
-        return remote(mine, mine, g_send.at[off - 1], g_recv.at[off - 1], (at_rep(off), pos))
+    def g_copy(piece, off):
+        n = piece * (NREP - 1) + off - 1
+        mine = listed.at[PIECES[piece], rep]
+        return remote(mine, mine, g_send.at[n], g_recv.at[n], (at_rep(off), pos))
 
     u_copy.wait()
     grads = u_vm[...].T
@@ -248,6 +237,25 @@
         x_copy(q, 0).start()
         x_copy(q, 2).start()
 
+    for copy in others[0:2]:
+        copy.wait()
+    lane8 = lax.broadcasted_iota(jnp.int32, (8, 128), 1)
+    row8 = lax.broadcasted_iota(jnp.int32, (8, 128), 0)
+    own = lane8 - (rep % 8) * 16
+    target = [
+        [jnp.where(k < cnt_ref[0, t], ids_ref[t, 0, k], -64) for k in range(SLOTS)] for t in range(2 * TILE_ROWS)
+    ]
+    codes_own = jnp.where((own >= 0) & (own < 16), -64, 0)
+    for k in range(SLOTS):
+        column = jnp.zeros((8, 128), jnp.int32)
+        for t in range(2 * TILE_ROWS):
+            column = jnp.where(row8 == t, target[t][k], column)
+        codes_own = jnp.where(own == k, column, codes_own)
+        codes_own = jnp.where(own == k + SLOTS, column + NBLK, codes_own)
+    code[...] = codes_own
+    codes[rep] = codes_own
+    stage[...] = jnp.zeros_like(stage)
+
     y_mid(0)
     y_mid(1)
     x_mid(0)
@@ -256,8 +264,6 @@
     x_mid(3)
     x_last(0)
     x_last(1)
-    for off in range(1, NREP):
-        c_copy(off).start()
 
     total = part[ORDER.index(0), :, 0:H1].astype(F32)
     for n in (6, 7, 4, 5):
@@ -268,11 +274,65 @@
         x1_copy(off).start()
     x_last(2)
     x_last(3)
+    for off in range(1, NREP):
+        c_copy(off).start()
+
+    for copy in others[2:]:
+        copy.wait()
+
+    row64 = lax.broadcasted_iota(jnp.int32, (EDGE, 128), 0)
+    lane64 = lax.broadcasted_iota(jnp.int32, (EDGE, 128), 1)
+    low_lanes = lane64 < EDGE
+    block64 = row64 % NBLK
+
+    def left(table, v):
+        out = []
+        for a in range(v.shape[0] // EDGE):
+            hi, lo = parts_of(v[a * EDGE : a * EDGE + EDGE])
+            out.append(dot(table, jnp.concatenate([hi, lo, hi], axis=0)))
+        return jnp.concatenate(out, axis=0)
+
+    keep = []
+
+    def list_and_send(piece, moment):
+        hi, lo = parts_of(moment)
+        coeffs = left(lf_vm[...], dot(jnp.concatenate([hi, lo, hi], axis=1), rf_vm[...])).astype(BF16).astype(F32)
+        first = PIECES[piece].start
+        for a in range(first, PIECES[piece].stop):
+            tile = coeffs[(a - first) * EDGE : (a - first) * EDGE + EDGE]
+            live = jnp.zeros((EDGE, 128), F32)
+            for k in range(SLOTS):
+                chosen = jnp.where(low_lanes, target[2 * a][k], target[2 * a + 1][k]) == block64
+                live = jnp.where(chosen, 1.0, live)
+                rows = jnp.where(chosen, tile, 0.0)
+                stage[a, k : k + 1] = jnp.sum(rows[0:NBLK], axis=0, keepdims=True)
+                stage[a, SLOTS + k : SLOTS + k + 1] = jnp.sum(rows[NBLK:EDGE], axis=0, keepdims=True)
+            keep.append(tile * live)
+            listed[a, rep] = stage[a].astype(BF16)
+        for off in REPLICAS:
+            g_copy(piece, off).start()
+
+    g1 = r1[x].astype(F32)
+    for off in range(1, NX):
+        x1_copy(off).wait_recv()
+        g1 += x1_slots[off - 1].astype(F32)
+    moment1 = 0.9 * mom_vm[0, 0:H1] + g1
+    list_and_send(0, moment1)
+    g2 = r2[ORDER.index(0)].astype(F32)
+    for off in range(1, NY):
+        y2_copy(off).wait_recv()
+        g2 += y2_slots[off - 1].astype(F32)
+    moment2 = 0.9 * mom_vm[0, H1:ROWS] + g2
+    list_and_send(1, moment2)
+
+    removed = jnp.concatenate(keep, axis=0).astype(BF16)
+    right_inv = ri_vm[...]
+    taken = left(li_vm[...], dot(jnp.concatenate([removed, removed], axis=1), right_inv[0:256]))
+    out_ref[1, 0:H1] = moment1 - taken[0:H1]
+    out_ref[1, H1:ROWS] = moment2 - taken[H1:ROWS]
 
     for off in range(1, NREP):
         c_copy(off).wait_recv()
-    row64 = lax.broadcasted_iota(jnp.int32, (EDGE, 128), 0)
-    lane64 = lax.broadcasted_iota(jnp.int32, (EDGE, 128), 1)
     for side in range(NREP // 8):
         tile = codes[8 * side]
         for r in range(1, 8):
@@ -281,57 +341,11 @@
             hit = (tile[t : t + 1] == row64).astype(F32).astype(BF16)
             spread_w[t // 2, EDGE * (t % 2) : EDGE * (t % 2) + EDGE, 128 * side : 128 * side + 128] = hit
 
-    for copy in others[2:]:
-        copy.wait()
-
-    g1 = r1[x].astype(F32)
-    for off in range(1, NX):
-        x1_copy(off).wait_recv()
-        g1 += x1_slots[off - 1].astype(F32)
-    moment_vm[0:H1] = 0.9 * mom_vm[0, 0:H1] + g1
-    g2 = r2[ORDER.index(0)].astype(F32)
-    for off in range(1, NY):
-        y2_copy(off).wait_recv()
-        g2 += y2_slots[off - 1].astype(F32)
-    moment_vm[H1:ROWS] = 0.9 * mom_vm[0, H1:ROWS] + g2
-    moment = moment_vm[...]
-
-    def left(table, v):
-        out = []
-        for a in range(TILE_ROWS):
-            hi, lo = parts_of(v[a * EDGE : a * EDGE + EDGE])
-            out.append(dot(table, jnp.concatenate([hi, lo, hi], axis=0)))
-        return jnp.concatenate(out, axis=0)
-
-    hi, lo = parts_of(moment)
-    coeffs = left(lf_vm[...], dot(jnp.concatenate([hi, lo, hi], axis=1), rf_vm[...])).astype(BF16).astype(F32)
-    low_lanes = lane64 < EDGE
-    block64 = row64 % NBLK
-    keep = []
-    stage[...] = jnp.zeros_like(stage)
-    for a in range(TILE_ROWS):
-        tile = coeffs[a * EDGE : a * EDGE + EDGE]
-        live = jnp.zeros((EDGE, 128), F32)
-        for k in range(SLOTS):
-            chosen = jnp.where(low_lanes, target[2 * a][k], target[2 * a + 1][k]) == block64
-            live = jnp.where(chosen, 1.0, live)
-            rows = jnp.where(chosen, tile, 0.0)
-            stage[a, k : k + 1] = jnp.sum(rows[0:NBLK], axis=0, keepdims=True)
-            stage[a, SLOTS + k : SLOTS + k + 1] = jnp.sum(rows[NBLK:EDGE], axis=0, keepdims=True)
-        keep.append(tile * live)
-    listed[:, rep] = stage[...].astype(BF16)
-    for off in range(1, NREP):
-        g_copy(off).start()
-
-    removed = jnp.concatenate(keep, axis=0).astype(BF16)
-    right_inv = ri_vm[...]
-    taken = left(li_vm[...], dot(jnp.concatenate([removed, removed], axis=1), right_inv[0:256]))
-    out_ref[1] = moment - taken
-
     for copy in started:
         copy.wait_send()
-    for off in range(1, NREP):
-        g_copy(off).wait_recv()
+    for piece in range(len(PIECES)):
+        for off in range(1, NREP):
+            g_copy(piece, off).wait_recv()
 
     summed = []
     for a in range(TILE_ROWS):
@@ -382,7 +396,6 @@
             pltpu.VMEM((TILE_ROWS, 2 * EDGE, NREP * 16), BF16),
             pltpu.VMEM((TILE_ROWS, NREP, 16, 128), BF16),
             pltpu.VMEM((TILE_ROWS, 16, 128), F32),
-            pltpu.VMEM((ROWS, FW), F32),
             dma((NY,)),
             dma((9,)),
             dma((8,)), dma((8,)),
@@ -390,7 +403,7 @@
             dma((NX - 1,)), dma((NX - 1,)),
             dma((NY - 1,)), dma((NY - 1,)),
             dma((NREP - 1,)), dma((NREP - 1,)),
-            dma((NREP - 1,)), dma((NREP - 1,)),
+            dma((len(PIECES) * (NREP - 1),)), dma((len(PIECES) * (NREP - 1),)),
         ],
         compiler_params=pltpu.CompilerParams(
             collective_id=0, has_side_effects=True, vmem_limit_bytes=60 * 1024 * 1024

time: 41.5 us -> 41 us (0.988)
  Pallas kernels: 40.1 us -> 39.5 us
    pallas_call x1, Pallas kernels: 40.1 us -> 39.5 us  [on_device(): pl.pallas_call(kernel, out_shape=pltpu.VMEM((2, ROWS, FW), F32), in_specs...]
where the time goes in v4:
time: 41 us; the launch traced here: 40.8 us
  Pallas kernels  39.5 us (96%)
  local copies, waits for them, and re-layouts  0.69 us (2%)
  between operations  0.64 us (2%)
    pallas_call x1, Pallas kernels, on_device(): pl.pallas_call(kernel, out_shape=pltpu.VMEM((2, ROWS, FW), F32), in_specs...  39.5 us

profile of v4, /device:TPU:1, one launch (start us, length us, event | category | flops | bytes accessed | tf_op | source)
XLA Modules:
  0.0 40.8 jit_solution(15308669511347469767)
XLA Ops:
  0.6 39.5 %shard_map.113 = f32[2,192,128]{2,1,0:T(8,128)S(1)} custom-call(bf16[256,6144]{1,0:T(8,128)(2,1)} %a_hbm.1, bf16[256,128]{1,0:T(8,128)(2,1)} %u_hbm.1, f32[1,192,128]{2,1,0:T(8,128)} %mom_hbm.1, f32[192,128]{1,0:T(8,128)} %w_hbm.1, s32[6,1,6]{2,1,0:T(1,128)} %bitcast.3, s32[1,6]{1,0:T(1,128)} %cnt_hbm.1, bf16[384,128]{1,0:T(8,128)(2,1)} %constant.8.clone.rf_hbm, ...), custom_call_target="tpu_custom_call" | custom-call | tf_op jit(solution)/shard_map/pallas_call | solution.py:371
  40.2 0.7 %fusion = (f32[1,192,128]{2,1,0:T(8,128)}, f32[192,128]{1,0:T(8,128)}) fusion(f32[2,192,128]{2,1,0:T(8,128)S(1)} %shard_map.113), kind=kLoop, calls=%fused_computation.1 | loop fusion | bytes 393216 | tf_op jit(solution)/shard_map/slice | solution.py:412

commit v5 on v4

--- a/solution.py
+++ b/solution.py
@@ -85,7 +85,7 @@
         return ((y + off) % NY) * NX + x
 
     def at_x(off):
-        return y * NX + (x + off) % NX
+        return y * NX + (x + NX + off) % NX
 
     def at_rep(off):
         return (rep + off) % NREP
@@ -166,7 +166,7 @@
         y_copy(4 + side).start()
 
     def x_way(q):
-        return 1 if q % 2 == 0 else -1
+        return 1 - 2 * ((q + rep) % 2)
 
     def x_copy(q, which):
         way = x_way(q)
@@ -177,13 +177,13 @@
         elif which == 1:
             src = x_slots.at[3 * q]
         else:
-            src = part.at[rows, (x - way) % NX, pl.ds(H1, H2)]
+            src = part.at[rows, (x + NX - way) % NX, pl.ds(H1, H2)]
             way = -way
         return remote(src, x_slots.at[n], x_send.at[n], x_recv.at[n], (rep, at_x(way)))
 
     def x_mid(q):
         x_copy(q, 0).wait_recv()
-        mine = part[2 * q : 2 * q + 2, (x + x_way(q)) % NX, H1:ROWS]
+        mine = part[2 * q : 2 * q + 2, (x + NX + x_way(q)) % NX, H1:ROWS]
         x_slots[3 * q] = (x_slots[3 * q].astype(F32) + mine.astype(F32)).astype(BF16)
         x_copy(q, 1).start()
 
@@ -343,25 +343,25 @@
 
     for copy in started:
         copy.wait_send()
+    lane1 = lax.broadcasted_iota(jnp.int32, (1, 128), 1) < EDGE
     for piece in range(len(PIECES)):
         for off in range(1, NREP):
             g_copy(piece, off).wait_recv()
-
-    summed = []
-    for a in range(TILE_ROWS):
-        rows = dot(spread_w[a], listed[a].reshape(NREP * 16, 128))
-        summed.append(jnp.where(low_lanes, rows[0:EDGE], rows[EDGE : 2 * EDGE]))
-    hi, lo = parts_of(jnp.concatenate(summed, axis=0))
-    update = left(li_vm[...], dot(jnp.concatenate([hi, hi, lo], axis=1), right_inv))
-    lane1 = lax.broadcasted_iota(jnp.int32, (1, 128), 1) < EDGE
-    for a in range(TILE_ROWS):
-        tile = update[a * EDGE : a * EDGE + EDGE]
-        squares = jnp.sum(tile * tile, axis=0, keepdims=True)
-        first = jnp.sum(jnp.where(lane1, squares, 0.0), axis=1, keepdims=True)
-        second = jnp.sum(jnp.where(lane1, 0.0, squares), axis=1, keepdims=True)
-        scale = lax.rsqrt(jnp.where(lane1, first, second) * (1.0 / (EDGE * EDGE)) + 1e-6)
-        span = slice(a * EDGE, a * EDGE + EDGE)
-        out_ref[0, span] = w_vm[span] - 0.25 * jnp.tanh(tile * scale)
+        first = PIECES[piece].start
+        summed = []
+        for a in range(first, PIECES[piece].stop):
+            rows = dot(spread_w[a], listed[a].reshape(NREP * 16, 128))
+            summed.append(jnp.where(low_lanes, rows[0:EDGE], rows[EDGE : 2 * EDGE]))
+        hi, lo = parts_of(jnp.concatenate(summed, axis=0))
+        update = left(li_vm[...], dot(jnp.concatenate([hi, hi, lo], axis=1), right_inv))
+        for a in range(first, PIECES[piece].stop):
+            tile = update[(a - first) * EDGE : (a - first) * EDGE + EDGE]
+            squares = jnp.sum(tile * tile, axis=0, keepdims=True)
+            low = jnp.sum(jnp.where(lane1, squares, 0.0), axis=1, keepdims=True)
+            high = jnp.sum(jnp.where(lane1, 0.0, squares), axis=1, keepdims=True)
+            scale = lax.rsqrt(jnp.where(lane1, low, high) * (1.0 / (EDGE * EDGE)) + 1e-6)
+            span = slice(a * EDGE, a * EDGE + EDGE)
+            out_ref[0, span] = w_vm[span] - 0.25 * jnp.tanh(tile * scale)
 
 
 def on_device(activations, unit_grads, momentum, weights, block_ids, block_counts):

time: 41 us -> 40.6 us (level)
  no operation moved by 1% of the time
where the time goes in v5:
time: 40.6 us; the launch traced here: 40.5 us
  Pallas kernels  39.1 us (96%)
  local copies, waits for them, and re-layouts  0.69 us (2%)
  between operations  0.64 us (2%)
    pallas_call x1, Pallas kernels, on_device(): pl.pallas_call(kernel, out_shape=pltpu.VMEM((2, ROWS, FW), F32), in_specs...  39.1 us

profile of v5, /device:TPU:1, one launch (start us, length us, event | category | flops | bytes accessed | tf_op | source)
XLA Modules:
  0.0 40.5 jit_solution(5016097337661212549)
XLA Ops:
  0.6 39.1 %shard_map.113 = f32[2,192,128]{2,1,0:T(8,128)S(1)} custom-call(bf16[256,6144]{1,0:T(8,128)(2,1)} %a_hbm.1, bf16[256,128]{1,0:T(8,128)(2,1)} %u_hbm.1, f32[1,192,128]{2,1,0:T(8,128)} %mom_hbm.1, f32[192,128]{1,0:T(8,128)} %w_hbm.1, s32[6,1,6]{2,1,0:T(1,128)} %bitcast.3, s32[1,6]{1,0:T(1,128)} %cnt_hbm.1, bf16[384,128]{1,0:T(8,128)(2,1)} %constant.8.clone.rf_hbm, ...), custom_call_target="tpu_custom_call" | custom-call | tf_op jit(solution)/shard_map/pallas_call | solution.py:371
  39.8 0.7 %fusion = (f32[1,192,128]{2,1,0:T(8,128)}, f32[192,128]{1,0:T(8,128)}) fusion(f32[2,192,128]{2,1,0:T(8,128)S(1)} %shard_map.113), kind=kLoop, calls=%fused_computation.1 | loop fusion | bytes 393216 | tf_op jit(solution)/shard_map/slice | solution.py:412

commit v6 on v5

--- a/solution.py
+++ b/solution.py
@@ -235,7 +235,8 @@
         if q == 3:
             y_copy(7).start()
         x_copy(q, 0).start()
-        x_copy(q, 2).start()
+        if q < 3:
+            x_copy(q, 2).start()
 
     for copy in others[0:2]:
         copy.wait()
@@ -257,9 +258,10 @@
     stage[...] = jnp.zeros_like(stage)
 
     y_mid(0)
+    x_mid(0)
     y_mid(1)
-    x_mid(0)
     x_mid(1)
+    x_copy(3, 2).start()
     x_mid(2)
     x_mid(3)
     x_last(0)

time: 40.6 us -> 41.1 us (1.012)
  Pallas kernels: 39.1 us -> 39.7 us
    pallas_call x1, Pallas kernels: 39.1 us -> 39.7 us  [on_device(): pl.pallas_call(kernel, out_shape=pltpu.VMEM((2, ROWS, FW), F32), in_specs...]
where the time goes in v6:
time: 41.1 us; the launch traced here: 41 us
  Pallas kernels  39.7 us (97%)
  local copies, waits for them, and re-layouts  0.69 us (2%)
  between operations  0.64 us (2%)
    pallas_call x1, Pallas kernels, on_device(): pl.pallas_call(kernel, out_shape=pltpu.VMEM((2, ROWS, FW), F32), in_specs...  39.7 us

profile of v6, /device:TPU:1, one launch (start us, length us, event | category | flops | bytes accessed | tf_op | source)
XLA Modules:
  0.0 41.0 jit_solution(1715796315464291399)
XLA Ops:
  0.6 39.7 %shard_map.113 = f32[2,192,128]{2,1,0:T(8,128)S(1)} custom-call(bf16[256,6144]{1,0:T(8,128)(2,1)} %a_hbm.1, bf16[256,128]{1,0:T(8,128)(2,1)} %u_hbm.1, f32[1,192,128]{2,1,0:T(8,128)} %mom_hbm.1, f32[192,128]{1,0:T(8,128)} %w_hbm.1, s32[6,1,6]{2,1,0:T(1,128)} %bitcast.3, s32[1,6]{1,0:T(1,128)} %cnt_hbm.1, bf16[384,128]{1,0:T(8,128)(2,1)} %constant.8.clone.rf_hbm, ...), custom_call_target="tpu_custom_call" | custom-call | tf_op jit(solution)/shard_map/pallas_call | solution.py:373
  40.3 0.7 %fusion = (f32[1,192,128]{2,1,0:T(8,128)}, f32[192,128]{1,0:T(8,128)}) fusion(f32[2,192,128]{2,1,0:T(8,128)S(1)} %shard_map.113), kind=kLoop, calls=%fused_computation.1 | loop fusion | bytes 393216 | tf_op jit(solution)/shard_map/slice | solution.py:414
